TPU v7x, 32 devices: a whole 2x2x4 slice. The times are simulated.
32 devices in a mesh: dp: 8 (over z, x), mp: 4 (over y, core).
Axes of the slice: x: 2, y: 2, z: 4, core: 2. Of those that a mesh axis runs over, the one named last changes fastest.
Arguments:
- image_embed: bfloat16 [4096, 1152], P(('dp', 'mp')), may hold values from -0.176776695 to 0.176776695
- text_embed: bfloat16 [4096, 1152], P(('dp', 'mp')), may hold values from -0.176776695 to 0.176776695
- log_scale: float32 [1], replicated, may hold values from 1.1 to 2.3
- logit_bias: float32 [1], replicated, may hold values from -3 to -1
Outputs:
- loss: float32 [1], replicated
- image_grad: float32 [4096, 1152], P(('dp', 'mp'))
- text_grad: float32 [4096, 1152], P(('dp', 'mp'))
All inputs are finite; a program needn't handle non-finite values.
Results may differ from a plain program's by a relative error of at most 0.0015.
Values may be sent and summed in bfloat16 or wider, within the bound.
A program may use at most 128 MiB of HBM per device.

v0:
```python
import functools

import jax
import jax.numpy as jnp
from jax import lax
from jax.experimental import pallas as pl
from jax.experimental.pallas import tpu as pltpu
from jax.sharding import PartitionSpec as P

STEPS = 2
MESH = pl.DeviceIdType.MESH
NT = (((1,), (1,)), ((), ()))


def unit_rows(raw):
    values = raw.astype(jnp.float32)
    norm = jnp.sqrt(jnp.sum(values * values, axis=1, keepdims=True) + 1e-06)
    return (values / norm, norm)


def back_norm(hat, raw):
    unit, norm = unit_rows(raw)
    return (hat - unit * jnp.sum(unit * hat, axis=1, keepdims=True)) / norm


def fold(values):
    rows, columns = values.shape
    tall = values[0:8]
    for r in range(8, rows, 8):
        tall = tall + values[r : r + 8]
    tile = tall[:, 0:128]
    for c in range(128, columns, 128):
        tile = tile + tall[:, c : c + 128]
    return tile


def kernel(
    n_dp, n_mp, image_hbm, text_hbm, log_scale_ref, bias_ref,
    loss_ref, image_grad_ref, text_grad_ref,
    image_ref, text_ref, texts, images, image_hat, text_hat, term_sum, group_terms, all_terms,
    load_sem, send_sem, row_sem, group_sem, all_sem,
):
    rows = image_ref.shape[0]
    chips, half = n_mp // 2, rows // 2
    g, m = lax.axis_index("dp"), lax.axis_index("mp")
    c, k = m // 2, lax.rem(m, 2)
    sibling = 2 * c + 1 - k
    towards = (lax.rem(g + 1, n_dp), lax.rem(g + n_dp - 1, n_dp))

    def same_core(d):
        return 2 * lax.rem(c + d, chips) + k

    def peer(d):
        return lax.rem(m + d, n_mp)

    def ring(d):
        return lax.rem(g + d, n_dp)

    loads = [
        pltpu.make_async_copy(text_hbm, text_ref, load_sem.at[0]),
        pltpu.make_async_copy(image_hbm, image_ref, load_sem.at[1]),
    ]
    for load in loads:
        load.start()

    partners = [(g, peer(d)) for d in range(1, n_mp)]
    partners += [(ring(d), m) for d in range(1, n_dp)]
    barrier = pltpu.get_barrier_semaphore()
    for partner in partners:
        pl.semaphore_signal(barrier, inc=1, device_id=partner, device_id_type=MESH)

    def block(which, step, index, part=None):
        ref = (texts, images)[which]
        if part is None:
            return ref.at[step, pl.ds(pl.multiple_of(index * rows, rows), rows), :]
        start = pl.multiple_of(index * rows + part * half, half)
        return ref.at[step, pl.ds(start, half), :]

    for which, ref in enumerate((text_ref, image_ref)):
        loads[which].wait()
        block(which, 0, m)[...] = unit_rows(ref[...])[0].astype(jnp.bfloat16)
    pl.semaphore_wait(barrier, len(partners))

    sends = []

    def push(src, dst, recv, device):
        copy = pltpu.make_async_remote_copy(
            src_ref=src, dst_ref=dst, send_sem=send_sem.at[len(sends)], recv_sem=recv,
            device_id=device, device_id_type=MESH,
        )
        copy.start()
        sends.append(copy)

    def await_copy(dst, recv):
        pltpu.make_async_remote_copy(
            src_ref=dst, dst_ref=dst, send_sem=send_sem.at[0], recv_sem=recv,
            device_id=(g, sibling), device_id_type=MESH,
        ).wait_recv()

    def send(which, step, index, part, device, to_step):
        push(block(which, step, index, part), block(which, to_step, index, part),
             row_sem.at[which, to_step, index, part], device)

    def take(which, step, index, part):
        await_copy(block(which, step, index, part), row_sem.at[which, step, index, part])

    def to_peers(which, step, index, part):
        for d in range(1, chips):
            send(which, step, index, part, (g, same_core(d)), step)

    def to_next(which, index, part):
        send(which, 0, index, part, (towards[which], m), 1)

    def to_sibling(which, step, index, part):
        send(which, step, index, part, (g, sibling), step)

    def start(*steps):
        first = len(sends)
        for step, *rest in steps:
            step(*rest)
        return first, len(sends)

    def sent(batch):
        for copy in sends[batch[0] : batch[1]]:
            copy.wait_send()
        waited.extend(range(*batch))

    waited = []
    text_0 = start((to_peers, 0, 0, m, 0), (to_next, 0, m, 1))
    text_1 = start((to_peers, 0, 0, m, 1), (to_next, 0, m, 0))
    for which in range(2):
        for part in range(2):
            to_sibling(which, 0, m, part)

    scale = jnp.exp(jnp.full((rows, 1), log_scale_ref[0], jnp.float32))
    bias = bias_ref[0]
    pair = 2 * rows
    done = [False, False]

    def score(which, step, d):
        low = block(1 - which, 0, m)
        hat = (image_hat, text_hat)[which]
        chip = lax.rem(c + d, chips)
        others = (texts, images)[which][step, pl.ds(pl.multiple_of(chip * pair, pair), pair), :]
        z = scale * lax.dot_general(low[...], others, NT, preferred_element_type=jnp.float32) + bias
        positive = None
        x = z
        if step == 0 and d == 0:
            row = lax.broadcasted_iota(jnp.int32, (rows, pair), 0)
            column = lax.broadcasted_iota(jnp.int32, (rows, pair), 1)
            positive = row + k * rows == column
            x = jnp.where(positive, -z, z)
        e = jnp.exp(-jnp.abs(x))
        coef = jnp.where(x >= 0, 1.0, e) / (1.0 + e)
        if positive is not None:
            coef = jnp.where(positive, -coef, coef)
        update = jnp.dot(coef.astype(jnp.bfloat16), others, preferred_element_type=jnp.float32)
        terms = fold(jnp.maximum(x, 0.0) + jnp.log1p(e)) if which == 0 else None
        if done[which]:
            hat[...] += update
            if which == 0:
                term_sum[...] += terms
        else:
            hat[...] = update
            if which == 0:
                term_sum[...] = terms
        done[which] = True

    def take_sibling(which, step, d):
        for part in range(2):
            take(which, step, 2 * lax.rem(c + d, chips) + 1 - k, part)

    for which in range(2):
        take_sibling(which, 0, 0)
        score(which, 0, 0)

    def arrive(which, part):
        for d in range(1, chips):
            take(which, 0, same_core(d), part)
            to_sibling(which, 0, same_core(d), part)
        take(which, 1, m, 1 - part)
        to_sibling(which, 1, m, 1 - part)

    def relay(which):
        steps = [(to_peers, which, 1, m, 1)]
        steps += [(to_next, which, same_core(d), 0) for d in range(1, chips)]
        return start(*steps)

    def last(which):
        for d in range(1, chips):
            for part in range(2):
                take(which, 1, same_core(d), part)
                to_sibling(which, 1, same_core(d), part)

    def score_first(which):
        for d in range(1, chips):
            take_sibling(which, 0, d)
            score(which, 0, d)
        take_sibling(which, 1, 0)
        score(which, 1, 0)

    sent(text_0)
    image_0 = start((to_peers, 1, 0, m, 0), (to_next, 1, m, 1))
    arrive(0, 0)
    sent(text_1)
    text_2 = relay(0)
    arrive(0, 1)
    score_first(0)
    sent(image_0)
    start((to_peers, 1, 0, m, 1), (to_next, 1, m, 0))
    arrive(1, 0)
    sent(text_2)
    relay(1)
    last(0)
    for d in range(1, chips):
        take_sibling(0, 1, d)
        score(0, 1, d)

    group_terms[m] = term_sum[...]
    for d in range(1, n_mp):
        push(group_terms.at[m], group_terms.at[m], group_sem.at[m], (g, peer(d)))
    image_grad_ref[...] = back_norm(scale * image_hat[...], image_ref[...])
    arrive(1, 1)
    for d in range(1, n_mp):
        await_copy(group_terms.at[peer(d)], group_sem.at[peer(d)])
    all_terms[g] = jnp.sum(group_terms[...], axis=0)
    for d in range(1, n_dp):
        push(all_terms.at[g], all_terms.at[g], all_sem.at[g], (ring(d), m))
    score_first(1)
    last(1)
    for d in range(1, chips):
        take_sibling(1, 1, d)
        score(1, 1, d)
    text_grad_ref[...] = back_norm(scale * text_hat[...], text_ref[...])
    for d in range(1, n_dp):
        await_copy(all_terms.at[ring(d)], all_sem.at[ring(d)])
    pair_count = n_dp * n_mp * rows * STEPS * n_mp * rows
    loss_ref[0] = jnp.sum(jnp.sum(all_terms[...], axis=0)) / pair_count
    for index, copy in enumerate(sends):
        if index not in waited:
            copy.wait_send()


def solution(mesh):
    n_dp, n_mp = mesh.shape["dp"], mesh.shape["mp"]

    def body(image_embed, text_embed, log_scale, logit_bias):
        rows, width = image_embed.shape
        chips = n_mp // 2
        others = chips - 1
        n_sends = 2 * (2 * others + 4) + 2 * (3 * others + 1) + 2 * (others + 1)
        n_sends += 2 * 2 * others + (n_mp - 1) + (n_dp - 1)
        vmem = pl.BlockSpec(memory_space=pltpu.VMEM)
        hbm = pl.BlockSpec(memory_space=pl.ANY)
        smem = pl.BlockSpec(memory_space=pltpu.SMEM)
        grad = jax.ShapeDtypeStruct((rows, width), jnp.float32)
        return pl.pallas_call(
            functools.partial(kernel, n_dp, n_mp),
            out_shape=(jax.ShapeDtypeStruct((1,), jnp.float32), grad, grad),
            in_specs=[hbm, hbm, smem, smem],
            out_specs=(smem, vmem, vmem),
            scratch_shapes=[
                pltpu.VMEM((rows, width), jnp.bfloat16),
                pltpu.VMEM((rows, width), jnp.bfloat16),
                pltpu.VMEM((2, n_mp * rows, width), jnp.bfloat16),
                pltpu.VMEM((2, n_mp * rows, width), jnp.bfloat16),
                pltpu.VMEM((rows, width), jnp.float32),
                pltpu.VMEM((rows, width), jnp.float32),
                pltpu.VMEM((8, 128), jnp.float32),
                pltpu.VMEM((n_mp, 8, 128), jnp.float32),
                pltpu.VMEM((n_dp, 8, 128), jnp.float32),
                pltpu.SemaphoreType.DMA((2,)),
                pltpu.SemaphoreType.DMA((n_sends,)),
                pltpu.SemaphoreType.DMA((2, 2, n_mp, 2)),
                pltpu.SemaphoreType.DMA((n_mp,)),
                pltpu.SemaphoreType.DMA((n_dp,)),
            ],
            compiler_params=pltpu.CompilerParams(
                collective_id=0, has_side_effects=True, vmem_limit_bytes=60 * 1024 * 1024
            ),
        )(image_embed, text_embed, log_scale, logit_bias)

    rows_spec = P(("dp", "mp"), None)
    return jax.shard_map(
        body,
        mesh=mesh,
        in_specs=(rows_spec, rows_spec, P(), P()),
        out_specs=(P(), rows_spec, rows_spec),
        check_vma=False,
    )
```

profile of v0, /device:TPU:0, one launch (start us, length us, event | category | flops | bytes accessed | tf_op | source)
XLA Modules:
  0.0 42.4 jit_solution(3758026012658809200)
XLA Ops:
  1.9 35.9 %shard_map.67 = (f32[1]{0:T(128)}, f32[128,1152]{1,0:T(8,128)}, f32[128,1152]{1,0:T(8,128)}) custom-call(bf16[128,1152]{1,0:T(8,128)(2,1)} %image_hbm.1, bf16[128,1152]{1,0:T(8,128)(2,1)} %text_hbm.1, f32[1]{0:T(128)S(6)} %copy.10.log_scale_ref, f32[1]{0:T(128)S(6)} %copy.11.bias_ref), custom_call_target="tpu_custom_call" | custom-call | tf_op jit(solution)/shard_map/pallas_call | solution.py:257
  38.4 0.0 copy-start
  38.5 2.0 %copy.13 = f32[128,1152]{1,0:T(8,128)} copy(f32[128,1152]{1,0:T(8,128)} %get-tuple-element.7) | data formatting | bytes 1179648
  40.4 0.0 copy-done
  40.4 0.8 %copy.14 = f32[128,1152]{1,0:T(8,128)} copy(f32[128,1152]{1,0:T(8,128)S(1)} %copy-done) | data formatting | bytes 1179648
Async XLA Ops:
  38.4 2.0 %copy-start = (f32[128,1152]{1,0:T(8,128)S(1)}, f32[128,1152]{1,0:T(8,128)}, u32[]{:S(2)}) copy-start(f32[128,1152]{1,0:T(8,128)} %get-tuple-element.8) | copy-start | bytes 1769476
where the time goes:
time: 42.6 us; the launch traced here: 42.4 us
  Pallas kernels  35.9 us (84%)
  between operations  3.67 us (9%)
  local copies, waits for them, and re-layouts  2.8 us (7%)
    pallas_call x1, Pallas kernels, body(): pl.pallas_call(functools.partial(kernel, n_dp, n_mp), out_shape=(jax.Shap...  35.9 us
    unnamed x4, local copies, waits for them, and re-layouts  2.8 us

commit v1 on v0

--- a/solution.py
+++ b/solution.py
@@ -76,9 +76,12 @@
         start = pl.multiple_of(index * rows + part * half, half)
         return ref.at[step, pl.ds(start, half), :]
 
-    for which, ref in enumerate((text_ref, image_ref)):
+    def normalise(which):
         loads[which].wait()
-        block(which, 0, m)[...] = unit_rows(ref[...])[0].astype(jnp.bfloat16)
+        low = unit_rows((text_ref, image_ref)[which][...])[0].astype(jnp.bfloat16)
+        block(which, 0, m)[...] = low
+
+    normalise(0)
     pl.semaphore_wait(barrier, len(partners))
 
     sends = []
@@ -114,23 +117,26 @@
     def to_sibling(which, step, index, part):
         send(which, step, index, part, (g, sibling), step)
 
-    def start(*steps):
+    def start(step, *rest):
         first = len(sends)
-        for step, *rest in steps:
-            step(*rest)
-        return first, len(sends)
-
-    def sent(batch):
-        for copy in sends[batch[0] : batch[1]]:
+        step(*rest)
+        return sends[first:]
+
+    def sent(copies):
+        for copy in copies:
             copy.wait_send()
-        waited.extend(range(*batch))
+        waited.extend(copies)
 
     waited = []
-    text_0 = start((to_peers, 0, 0, m, 0), (to_next, 0, m, 1))
-    text_1 = start((to_peers, 0, 0, m, 1), (to_next, 0, m, 0))
-    for which in range(2):
-        for part in range(2):
-            to_sibling(which, 0, m, part)
+    group_copies, next_copies = [], []
+    for part in range(2):
+        group_copies.append(start(to_peers, 0, 0, m, part))
+        next_copies.append(start(to_next, 0, m, 1 - part))
+    for part in range(2):
+        to_sibling(0, 0, m, part)
+    normalise(1)
+    for part in range(2):
+        to_sibling(1, 0, m, part)
 
     scale = jnp.exp(jnp.full((rows, 1), log_scale_ref[0], jnp.float32))
     bias = bias_ref[0]
@@ -177,14 +183,13 @@
     def arrive(which, part):
         for d in range(1, chips):
             take(which, 0, same_core(d), part)
+            if part == 0:
+                to_next(which, same_core(d), 0)
             to_sibling(which, 0, same_core(d), part)
         take(which, 1, m, 1 - part)
+        if part == 0:
+            to_peers(which, 1, m, 1)
         to_sibling(which, 1, m, 1 - part)
-
-    def relay(which):
-        steps = [(to_peers, which, 1, m, 1)]
-        steps += [(to_next, which, same_core(d), 0) for d in range(1, chips)]
-        return start(*steps)
 
     def last(which):
         for d in range(1, chips):
@@ -199,18 +204,14 @@
         take_sibling(which, 1, 0)
         score(which, 1, 0)
 
-    sent(text_0)
-    image_0 = start((to_peers, 1, 0, m, 0), (to_next, 1, m, 1))
-    arrive(0, 0)
-    sent(text_1)
-    text_2 = relay(0)
-    arrive(0, 1)
+    for part in range(2):
+        sent(group_copies[part])
+        to_peers(1, 0, m, part)
+        sent(next_copies[part])
+        to_next(1, m, 1 - part)
+        arrive(0, part)
+    arrive(1, 0)
     score_first(0)
-    sent(image_0)
-    start((to_peers, 1, 0, m, 1), (to_next, 1, m, 0))
-    arrive(1, 0)
-    sent(text_2)
-    relay(1)
     last(0)
     for d in range(1, chips):
         take_sibling(0, 1, d)
@@ -219,7 +220,7 @@
     group_terms[m] = term_sum[...]
     for d in range(1, n_mp):
         push(group_terms.at[m], group_terms.at[m], group_sem.at[m], (g, peer(d)))
-    image_grad_ref[...] = back_norm(scale * image_hat[...], image_ref[...])
+    image_grad_ref[...] = back_norm(image_hat[...], image_ref[...])
     arrive(1, 1)
     for d in range(1, n_mp):
         await_copy(group_terms.at[peer(d)], group_sem.at[peer(d)])
@@ -231,13 +232,13 @@
     for d in range(1, chips):
         take_sibling(1, 1, d)
         score(1, 1, d)
-    text_grad_ref[...] = back_norm(scale * text_hat[...], text_ref[...])
+    text_grad_ref[...] = back_norm(text_hat[...], text_ref[...])
     for d in range(1, n_dp):
         await_copy(all_terms.at[ring(d)], all_sem.at[ring(d)])
     pair_count = n_dp * n_mp * rows * STEPS * n_mp * rows
     loss_ref[0] = jnp.sum(jnp.sum(all_terms[...], axis=0)) / pair_count
-    for index, copy in enumerate(sends):
-        if index not in waited:
+    for copy in sends:
+        if not any(copy is other for other in waited):
             copy.wait_send()
 
 
@@ -254,7 +255,7 @@
         hbm = pl.BlockSpec(memory_space=pl.ANY)
         smem = pl.BlockSpec(memory_space=pltpu.SMEM)
         grad = jax.ShapeDtypeStruct((rows, width), jnp.float32)
-        return pl.pallas_call(
+        loss, image_grad, text_grad = pl.pallas_call(
             functools.partial(kernel, n_dp, n_mp),
             out_shape=(jax.ShapeDtypeStruct((1,), jnp.float32), grad, grad),
             in_specs=[hbm, hbm, smem, smem],
@@ -279,6 +280,8 @@
                 collective_id=0, has_side_effects=True, vmem_limit_bytes=60 * 1024 * 1024
             ),
         )(image_embed, text_embed, log_scale, logit_bias)
+        scale = jnp.exp(log_scale[0])
+        return loss, scale * image_grad, scale * text_grad
 
     rows_spec = P(("dp", "mp"), None)
     return jax.shard_map(

time: 42.6 us -> 42 us (0.986)
  local copies, waits for them, and re-layouts: 2.8 us -> 0 us
  other arithmetic: 0 us -> 2.33 us
    unnamed x4 -> x0, local copies, waits for them, and re-layouts: 2.8 us -> none
    mul x0 -> x1, other arithmetic: none -> 2.33 us  [body(): return (loss, scale * image_grad, scale * text_grad)]
where the time goes in v1:
time: 42 us; the launch traced here: 41.8 us
  Pallas kernels  35.8 us (85%)
  between operations  3.71 us (9%)
  other arithmetic  2.33 us (6%)
    pallas_call x1, Pallas kernels, body(): pl.pallas_call(functools.partial(kernel, n_dp, n_mp), out_shape=(jax.Shap...  35.8 us
    mul x1, other arithmetic, body(): return (loss, scale * image_grad, scale * text_grad)  2.33 us

profile of v1, /device:TPU:0, one launch (start us, length us, event | category | flops | bytes accessed | tf_op | source)
XLA Modules:
  0.0 41.8 jit_solution(1328412140796022093)
XLA Ops:
  2.0 35.8 %shard_map.67 = (f32[1]{0:T(128)}, f32[128,1152]{1,0:T(8,128)}, f32[128,1152]{1,0:T(8,128)}) custom-call(bf16[128,1152]{1,0:T(8,128)(2,1)} %image_hbm.1, bf16[128,1152]{1,0:T(8,128)(2,1)} %text_hbm.1, f32[1]{0:T(128)S(6)} %copy.8.log_scale_ref, f32[1]{0:T(128)S(6)} %copy.9.bias_ref), custom_call_target="tpu_custom_call" | custom-call | tf_op jit(solution)/shard_map/pallas_call | solution.py:258
  37.7 2.3 %broadcast_multiply_fusion = (f32[128,1152]{1,0:T(8,128)}, f32[128,1152]{1,0:T(8,128)}) fusion(f32[128,1152]{1,0:T(8,128)} %get-tuple-element.8, f32[]{:T(128)} %bitcast, f32[128,1152]{1,0:T(8,128)} %get-tuple-element.7), kind=kLoop, calls=%fused_computation | loop fusion | flops 294912 | bytes 2359300 | tf_op jit(solution)/shard_map/mul | solution.py:284

commit v2 on v1

--- a/solution.py
+++ b/solution.py
@@ -84,15 +84,16 @@
     normalise(0)
     pl.semaphore_wait(barrier, len(partners))
 
-    sends = []
+    sends, held = [], []
 
     def push(src, dst, recv, device):
         copy = pltpu.make_async_remote_copy(
             src_ref=src, dst_ref=dst, send_sem=send_sem.at[len(sends)], recv_sem=recv,
             device_id=device, device_id_type=MESH,
         )
-        copy.start()
         sends.append(copy)
+        if not held:
+            copy.start()
 
     def await_copy(dst, recv):
         pltpu.make_async_remote_copy(
@@ -117,10 +118,19 @@
     def to_sibling(which, step, index, part):
         send(which, step, index, part, (g, sibling), step)
 
-    def start(step, *rest):
+    def made(step, *rest):
+        held.append(True)
         first = len(sends)
         step(*rest)
+        held.pop()
         return sends[first:]
+
+    def start_both(one, two):
+        for core, order in enumerate((one + two, two + one)):
+            @pl.when(k == core)
+            def _():
+                for copy in order:
+                    copy.start()
 
     def sent(copies):
         for copy in copies:
@@ -130,8 +140,9 @@
     waited = []
     group_copies, next_copies = [], []
     for part in range(2):
-        group_copies.append(start(to_peers, 0, 0, m, part))
-        next_copies.append(start(to_next, 0, m, 1 - part))
+        group_copies.append(made(to_peers, 0, 0, m, part))
+        next_copies.append(made(to_next, 0, m, 1 - part))
+        start_both(group_copies[part], next_copies[part])
     for part in range(2):
         to_sibling(0, 0, m, part)
     normalise(1)
@@ -143,11 +154,14 @@
     pair = 2 * rows
     done = [False, False]
 
-    def score(which, step, d):
+    def score(which, step, d, core=None):
         low = block(1 - which, 0, m)
         hat = (image_hat, text_hat)[which]
         chip = lax.rem(c + d, chips)
-        others = (texts, images)[which][step, pl.ds(pl.multiple_of(chip * pair, pair), pair), :]
+        if core is None:
+            others = (texts, images)[which][step, pl.ds(pl.multiple_of(chip * pair, pair), pair), :]
+        else:
+            others = block(which, step, 2 * chip + core)[...]
         z = scale * lax.dot_general(low[...], others, NT, preferred_element_type=jnp.float32) + bias
         positive = None
         x = z
@@ -206,16 +220,16 @@
 
     for part in range(2):
         sent(group_copies[part])
-        to_peers(1, 0, m, part)
         sent(next_copies[part])
-        to_next(1, m, 1 - part)
+        start_both(made(to_peers, 1, 0, m, part), made(to_next, 1, m, 1 - part))
         arrive(0, part)
     arrive(1, 0)
     score_first(0)
     last(0)
     for d in range(1, chips):
+        score(0, 1, d, k)
         take_sibling(0, 1, d)
-        score(0, 1, d)
+        score(0, 1, d, 1 - k)
 
     group_terms[m] = term_sum[...]
     for d in range(1, n_mp):
@@ -230,8 +244,9 @@
     score_first(1)
     last(1)
     for d in range(1, chips):
+        score(1, 1, d, k)
         take_sibling(1, 1, d)
-        score(1, 1, d)
+        score(1, 1, d, 1 - k)
     text_grad_ref[...] = back_norm(text_hat[...], text_ref[...])
     for d in range(1, n_dp):
         await_copy(all_terms.at[ring(d)], all_sem.at[ring(d)])

time: 42 us -> 42 us (level)
  no operation moved by 1% of the time
where the time goes in v2:
time: 42 us; the launch traced here: 41.8 us
  Pallas kernels  35.8 us (85%)
  between operations  3.71 us (9%)
  other arithmetic  2.33 us (6%)
    pallas_call x1, Pallas kernels, body(): pl.pallas_call(functools.partial(kernel, n_dp, n_mp), out_shape=(jax.Shap...  35.8 us
    mul x1, other arithmetic, body(): return (loss, scale * image_grad, scale * text_grad)  2.33 us

profile of v2, /device:TPU:0, one launch (start us, length us, event | category | flops | bytes accessed | tf_op | source)
XLA Modules:
  0.0 41.8 jit_solution(6473558784244372587)
XLA Ops:
  2.0 35.8 %shard_map.67 = (f32[1]{0:T(128)}, f32[128,1152]{1,0:T(8,128)}, f32[128,1152]{1,0:T(8,128)}) custom-call(bf16[128,1152]{1,0:T(8,128)(2,1)} %image_hbm.1, bf16[128,1152]{1,0:T(8,128)(2,1)} %text_hbm.1, f32[1]{0:T(128)S(6)} %copy.8.log_scale_ref, f32[1]{0:T(128)S(6)} %copy.9.bias_ref), custom_call_target="tpu_custom_call" | custom-call | tf_op jit(solution)/shard_map/pallas_call | solution.py:273
  37.8 2.3 %broadcast_multiply_fusion = (f32[128,1152]{1,0:T(8,128)}, f32[128,1152]{1,0:T(8,128)}) fusion(f32[128,1152]{1,0:T(8,128)} %get-tuple-element.8, f32[]{:T(128)} %bitcast, f32[128,1152]{1,0:T(8,128)} %get-tuple-element.7), kind=kLoop, calls=%fused_computation | loop fusion | flops 294912 | bytes 2359300 | tf_op jit(solution)/shard_map/mul | solution.py:299

commit v3 on v2

--- a/solution.py
+++ b/solution.py
@@ -41,7 +41,7 @@
     load_sem, send_sem, row_sem, group_sem, all_sem,
 ):
     rows = image_ref.shape[0]
-    chips, half = n_mp // 2, rows // 2
+    chips, cut = n_mp // 2, rows * 3 // 8
     g, m = lax.axis_index("dp"), lax.axis_index("mp")
     c, k = m // 2, lax.rem(m, 2)
     sibling = 2 * c + 1 - k
@@ -73,8 +73,8 @@
         ref = (texts, images)[which]
         if part is None:
             return ref.at[step, pl.ds(pl.multiple_of(index * rows, rows), rows), :]
-        start = pl.multiple_of(index * rows + part * half, half)
-        return ref.at[step, pl.ds(start, half), :]
+        start = pl.multiple_of(index * rows + part * cut, 16)
+        return ref.at[step, pl.ds(start, (cut, rows - cut)[part]), :]
 
     def normalise(which):
         loads[which].wait()

time: 42 us -> 41.2 us (0.981)
  Pallas kernels: 35.8 us -> 35 us
    pallas_call x1, Pallas kernels: 35.8 us -> 35 us  [body(): pl.pallas_call(functools.partial(kernel, n_dp, n_mp), out_shape=(jax.Shap...]
where the time goes in v3:
time: 41.2 us; the launch traced here: 41 us
  Pallas kernels  35 us (85%)
  between operations  3.71 us (9%)
  other arithmetic  2.33 us (6%)
    pallas_call x1, Pallas kernels, body(): pl.pallas_call(functools.partial(kernel, n_dp, n_mp), out_shape=(jax.Shap...  35 us
    mul x1, other arithmetic, body(): return (loss, scale * image_grad, scale * text_grad)  2.33 us

profile of v3, /device:TPU:0, one launch (start us, length us, event | category | flops | bytes accessed | tf_op | source)
XLA Modules:
  0.0 41.0 jit_solution(8840593765720879320)
XLA Ops:
  2.0 35.0 %shard_map.67 = (f32[1]{0:T(128)}, f32[128,1152]{1,0:T(8,128)}, f32[128,1152]{1,0:T(8,128)}) custom-call(bf16[128,1152]{1,0:T(8,128)(2,1)} %image_hbm.1, bf16[128,1152]{1,0:T(8,128)(2,1)} %text_hbm.1, f32[1]{0:T(128)S(6)} %copy.8.log_scale_ref, f32[1]{0:T(128)S(6)} %copy.9.bias_ref), custom_call_target="tpu_custom_call" | custom-call | tf_op jit(solution)/shard_map/pallas_call | solution.py:273
  36.9 2.3 %broadcast_multiply_fusion = (f32[128,1152]{1,0:T(8,128)}, f32[128,1152]{1,0:T(8,128)}) fusion(f32[128,1152]{1,0:T(8,128)} %get-tuple-element.8, f32[]{:T(128)} %bitcast, f32[128,1152]{1,0:T(8,128)} %get-tuple-element.7), kind=kLoop, calls=%fused_computation | loop fusion | flops 294912 | bytes 2359300 | tf_op jit(solution)/shard_map/mul | solution.py:299

commit v4 on v3

--- a/solution.py
+++ b/solution.py
@@ -41,7 +41,7 @@
     load_sem, send_sem, row_sem, group_sem, all_sem,
 ):
     rows = image_ref.shape[0]
-    chips, cut = n_mp // 2, rows * 3 // 8
+    chips, cut = n_mp // 2, rows // 8
     g, m = lax.axis_index("dp"), lax.axis_index("mp")
     c, k = m // 2, lax.rem(m, 2)
     sibling = 2 * c + 1 - k

time: 41.2 us -> 44.4 us (1.078)
  Pallas kernels: 35 us -> 38.2 us
    pallas_call x1, Pallas kernels: 35 us -> 38.2 us  [body(): pl.pallas_call(functools.partial(kernel, n_dp, n_mp), out_shape=(jax.Shap...]
where the time goes in v4:
time: 44.4 us; the launch traced here: 44.2 us
  Pallas kernels  38.2 us (86%)
  between operations  3.71 us (8%)
  other arithmetic  2.33 us (5%)
    pallas_call x1, Pallas kernels, body(): pl.pallas_call(functools.partial(kernel, n_dp, n_mp), out_shape=(jax.Shap...  38.2 us
    mul x1, other arithmetic, body(): return (loss, scale * image_grad, scale * text_grad)  2.33 us

profile of v4, /device:TPU:0, one launch (start us, length us, event | category | flops | bytes accessed | tf_op | source)
XLA Modules:
  0.0 44.2 jit_solution(11932356459964341514)
XLA Ops:
  2.0 38.2 %shard_map.67 = (f32[1]{0:T(128)}, f32[128,1152]{1,0:T(8,128)}, f32[128,1152]{1,0:T(8,128)}) custom-call(bf16[128,1152]{1,0:T(8,128)(2,1)} %image_hbm.1, bf16[128,1152]{1,0:T(8,128)(2,1)} %text_hbm.1, f32[1]{0:T(128)S(6)} %copy.8.log_scale_ref, f32[1]{0:T(128)S(6)} %copy.9.bias_ref), custom_call_target="tpu_custom_call" | custom-call | tf_op jit(solution)/shard_map/pallas_call | solution.py:273
  40.2 2.3 %broadcast_multiply_fusion = (f32[128,1152]{1,0:T(8,128)}, f32[128,1152]{1,0:T(8,128)}) fusion(f32[128,1152]{1,0:T(8,128)} %get-tuple-element.8, f32[]{:T(128)} %bitcast, f32[128,1152]{1,0:T(8,128)} %get-tuple-element.7), kind=kLoop, calls=%fused_computation | loop fusion | flops 294912 | bytes 2359300 | tf_op jit(solution)/shard_map/mul | solution.py:299

commit v5 on v3

--- a/solution.py
+++ b/solution.py
@@ -220,7 +220,6 @@
 
     for part in range(2):
         sent(group_copies[part])
-        sent(next_copies[part])
         start_both(made(to_peers, 1, 0, m, part), made(to_next, 1, m, 1 - part))
         arrive(0, part)
     arrive(1, 0)

time: 41.2 us -> 42.7 us (1.036)
  Pallas kernels: 35 us -> 36.5 us
    pallas_call x1, Pallas kernels: 35 us -> 36.5 us  [body(): pl.pallas_call(functools.partial(kernel, n_dp, n_mp), out_shape=(jax.Shap...]
where the time goes in v5:
time: 42.7 us; the launch traced here: 42.5 us
  Pallas kernels  36.5 us (85%)
  between operations  3.71 us (9%)
  other arithmetic  2.33 us (5%)
    pallas_call x1, Pallas kernels, body(): pl.pallas_call(functools.partial(kernel, n_dp, n_mp), out_shape=(jax.Shap...  36.5 us
    mul x1, other arithmetic, body(): return (loss, scale * image_grad, scale * text_grad)  2.33 us

profile of v5, /device:TPU:0, one launch (start us, length us, event | category | flops | bytes accessed | tf_op | source)
XLA Modules:
  0.0 42.5 jit_solution(16206511011182354047)
XLA Ops:
  2.0 36.5 %shard_map.67 = (f32[1]{0:T(128)}, f32[128,1152]{1,0:T(8,128)}, f32[128,1152]{1,0:T(8,128)}) custom-call(bf16[128,1152]{1,0:T(8,128)(2,1)} %image_hbm.1, bf16[128,1152]{1,0:T(8,128)(2,1)} %text_hbm.1, f32[1]{0:T(128)S(6)} %copy.8.log_scale_ref, f32[1]{0:T(128)S(6)} %copy.9.bias_ref), custom_call_target="tpu_custom_call" | custom-call | tf_op jit(solution)/shard_map/pallas_call | solution.py:272
  38.5 2.3 %broadcast_multiply_fusion = (f32[128,1152]{1,0:T(8,128)}, f32[128,1152]{1,0:T(8,128)}) fusion(f32[128,1152]{1,0:T(8,128)} %get-tuple-element.8, f32[]{:T(128)} %bitcast, f32[128,1152]{1,0:T(8,128)} %get-tuple-element.7), kind=kLoop, calls=%fused_computation | loop fusion | flops 294912 | bytes 2359300 | tf_op jit(solution)/shard_map/mul | solution.py:298
